TPU v7x, 32 devices: a whole 2x2x4 slice. The times are simulated.
32 devices in a mesh: groups: 2 (over x), dev: 8 (over z, y), sub: 2 (over core).
Axes of the slice: x: 2, y: 2, z: 4, core: 2. Of those that a mesh axis runs over, the one named last changes fastest.
Arguments:
- tokens: bfloat16 [4096, 7168], P(('groups', 'dev', 'sub')), parts along dimension 0, may hold values from -6 to 6
- expert_ids: int32 [4096, 8], P(('groups', 'dev', 'sub')), parts along dimension 0, may hold values from 0 to 255, all different within a row; in each aligned block of 128 rows (0 to 127, 128 to 255, ...) at most 6 rows name the same one
- gate_values: float32 [4096, 8], P(('groups', 'dev', 'sub')), parts along dimension 0, may hold values from 0.05 to 1
- gate_proj: bfloat16 [16, 7168, 128], P(('dev', 'sub')), may hold values from -0.0625 to 0.0625
- up_proj: bfloat16 [16, 7168, 128], P(('dev', 'sub')), may hold values from -0.0625 to 0.0625
- down_proj: bfloat16 [16, 128, 7168], P(('dev', 'sub')), may hold values from -0.125 to 0.125
Outputs:
- moe_out: bfloat16 [4096, 7168], P(('groups', 'dev', 'sub')), parts along dimension 0
There are 2 independent parts, one for each index of `groups`. A program takes and returns all parts, laid end to end along the dimension named above; an argument that names none is the same for every part. Nothing has to cross between parts.
Inputs may be any that keep to these rules, and one draw needn't show every extreme that they name: `expert_ids`: each row names 8 different experts; within the 128 rows of one device no expert is named by more than 6 rows.
All inputs are finite; a program needn't handle non-finite values.
Results may differ from a plain program's by a relative error of at most 0.0058.
Values may be sent and summed in bfloat16 or wider, within the bound.
A program may use at most 128 MiB of HBM per device.

v0:
```python
import jax
import jax.numpy as jnp
from jax import lax
from jax.sharding import PartitionSpec as P

SH = 16
CAP = 6


def plan(expert_ids, gate_values, window):
    experts = jnp.arange(window, dtype=jnp.int32)
    matches = expert_ids[:, :, None] == experts[None, None, :]
    counts = jnp.sum(matches.astype(jnp.int32), axis=1)
    weight = jnp.sum(
        jnp.where(matches, gate_values[:, :, None], jnp.zeros_like(gate_values[:, :, None])), axis=1
    )
    ranking = jnp.cumsum(counts, axis=0) - 1
    slot_ids = jnp.arange(CAP, dtype=jnp.int32)
    chosen = (counts.T[:, None, :] == 1) & (ranking.T[:, None, :] == slot_ids[None, :, None])
    return (chosen, weight)


def local(tokens, expert_ids, gate_values, gate_proj, up_proj, down_proj):
    devices = lax.axis_size("dev") * lax.axis_size("sub")
    window = devices // SH
    model_width = tokens.shape[1]
    chosen, weight = plan(expert_ids, gate_values, window)
    picked = chosen.astype(jnp.bfloat16).reshape(window * CAP, tokens.shape[0])
    outbound = jnp.dot(picked, tokens, preferred_element_type=jnp.float32).astype(jnp.bfloat16)
    outbound = outbound.reshape(window, 1, CAP, model_width)
    sendbuf = jnp.broadcast_to(outbound, (window, SH, CAP, model_width)).reshape(
        devices, CAP, model_width
    )
    arrived = lax.all_to_all(sendbuf, ("dev", "sub"), split_axis=0, concat_axis=0, tiled=True)
    row_block = arrived.reshape(devices * CAP, model_width)
    gate_act = jnp.dot(row_block, gate_proj[0], preferred_element_type=jnp.float32)
    up_act = jnp.dot(row_block, up_proj[0], preferred_element_type=jnp.float32)
    hidden = (jax.nn.silu(gate_act) * up_act).astype(jnp.bfloat16)
    partial_value = jnp.dot(hidden, down_proj[0], preferred_element_type=jnp.float32).astype(
        jnp.bfloat16
    )
    returned = lax.all_to_all(
        partial_value.reshape(devices, CAP, model_width),
        ("dev", "sub"),
        split_axis=0,
        concat_axis=0,
        tiled=True,
    )
    merged = jnp.sum(returned.reshape(window, SH, CAP, model_width).astype(jnp.float32), axis=1)
    combine = (chosen.astype(jnp.float32) * weight.T[:, None, :]).reshape(
        window * CAP, tokens.shape[0]
    )
    moe_out = jnp.dot(
        combine.T,
        merged.reshape(window * CAP, model_width),
        precision=lax.Precision.HIGHEST,
        preferred_element_type=jnp.float32,
    )
    return moe_out.astype(jnp.bfloat16)


def solution(mesh):
    placed = (
        P(("groups", "dev", "sub"), None),
        P(("groups", "dev", "sub"), None),
        P(("groups", "dev", "sub"), None),
        P(("dev", "sub"), None, None),
        P(("dev", "sub"), None, None),
        P(("dev", "sub"), None, None),
    )
    return jax.shard_map(
        local,
        mesh=mesh,
        in_specs=placed,
        out_specs=P(("groups", "dev", "sub"), None),
        check_vma=False,
    )
```

profile of v0, /device:TPU:0, one launch (start us, length us, event | category | flops | bytes accessed | tf_op | source)
XLA Modules:
  0.0 114.7 jit_solution(13393264071294892745)
XLA Ops:
  0.0 0.0 copy-start
  0.0 0.9 select_reduce_fusion
  0.9 0.1 copy.8
  1.0 0.2 reduce-window.7
  1.2 0.1 add_reduce_fusion
  1.3 1.8 %convolution_convert_fusion.2 = bf16[6,7168]{1,0:T(8,128)(2,1)S(1)} fusion(bf16[128,7168]{1,0:T(8,128)(2,1)} %param.6, s32[128]{0:T(128)S(1)} %add_reduce_fusion, pred[128]{0:T(512)(128)(4,1)S(1)} %broadcast_compare_fusion.1), kind=kOutput, calls=%fused_computation.2 | convolution fusion | flops 11054592 | bytes 1921664 | tf_op jit(solution)/shard_map/dot_general | solution.py:29
  3.1 0.2 reshape.128
  3.3 50.0 %all_to_all.10 = bf16[16,6,7168]{2,1,0:T(8,128)(2,1)} all-to-all(bf16[16,6,7168]{2,1,0:T(8,128)(2,1)S(1)} %reshape.128), channel_id=1, replica_groups=mesh['groups'=2,'dev'=8,'sub'=2] {'dev','sub'}, dimensions={0} | all-to-all | bytes 2752512 | tf_op jit(solution)/shard_map/all_to_all | solution.py:34
  53.4 1.7 %reshape.129 = bf16[96,7168]{1,0:T(8,128)(2,1)S(1)} reshape(bf16[16,6,7168]{2,1,0:T(8,128)(2,1)} %all_to_all.10) | data formatting | bytes 2752512 | tf_op jit(solution)/shard_map/reshape | solution.py:35
  55.1 2.0 %fusion.3 = f32[96,128]{1,0:T(8,128)S(1)} fusion(bf16[96,7168]{1,0:T(8,128)(2,1)S(1)} %reshape.129, bf16[1,7168,128]{2,1,0:T(8,128)(2,1)} %param.9), kind=kOutput, calls=%fused_computation.7 | convolution fusion | flops 176160768 | bytes 3260416 | tf_op jit(solution)/shard_map/dot_general | solution.py:36
  57.1 0.0 copy-done
  57.1 3.6 %convolution_convert_fusion.1 = bf16[96,7168]{1,0:T(8,128)(2,1)} fusion(bf16[1,128,7168]{2,1,0:T(8,128)(2,1)S(1)} %copy-done, bf16[96,7168]{1,0:T(8,128)(2,1)S(1)} %reshape.129, bf16[1,7168,128]{2,1,0:T(8,128)(2,1)} %param.10, f32[96,128]{1,0:T(8,128)S(1)} %fusion.3), kind=kOutput, calls=%fused_computation.1 | convolution fusion | flops 353083392 | bytes 6471680 | tf_op jit(solution)/shard_map/dot_general | solution.py:39
  60.7 2.6 %reshape.130 = bf16[16,6,7168]{2,1,0:T(8,128)(2,1)} reshape(bf16[96,7168]{1,0:T(8,128)(2,1)} %convolution_convert_fusion.1) | data formatting | bytes 2752512 | tf_op jit(solution)/shard_map/reshape | solution.py:43
  63.3 46.8 %all_to_all.11 = bf16[16,6,7168]{2,1,0:T(8,128)(2,1)S(1)} all-to-all(bf16[16,6,7168]{2,1,0:T(8,128)(2,1)} %reshape.130), channel_id=1, replica_groups=mesh['groups'=2,'dev'=8,'sub'=2] {'dev','sub'}, dimensions={0} | all-to-all | bytes 2752512 | tf_op jit(solution)/shard_map/all_to_all | solution.py:42
  110.0 0.4 convert_reduce_fusion
  110.4 4.3 %convolution_convert_fusion = bf16[128,7168]{1,0:T(8,128)(2,1)} fusion(f32[6,7168]{1,0:T(8,128)S(1)} %convert_reduce_fusion, f32[128]{0:T(128)S(1)} %get-tuple-element.5, s32[128]{0:T(128)S(1)} %add_reduce_fusion, pred[128]{0:T(512)(128)(4,1)S(1)} %broadcast_compare_fusion.1), kind=kOutput, calls=%fused_computation | convolution fusion | flops 66980096 | bytes 2008192 | tf_op jit(solution)/shard_map/dot_general | solution.py:53
  (2 shorter events, 0.0 us)
Async XLA Ops:
  0.0 57.1 %copy-start = (bf16[1,128,7168]{2,1,0:T(8,128)(2,1)S(1)}, bf16[1,128,7168]{2,1,0:T(8,128)(2,1)}, u32[]{:S(2)}) copy-start(bf16[1,128,7168]{2,1,0:T(8,128)(2,1)} %param.11) | copy-start | bytes 5505028
where the time goes:
time: 115 us
  blocking collectives  96.8 us (84%)
  matrix products  11.7 us (10%)
  local copies, waits for them, and re-layouts  4.59 us (4%)
  other arithmetic  1.53 us (1%)
    all_to_all x1, blocking collectives, local(): lax.all_to_all(sendbuf, ('dev', 'sub'), split_axis=0, concat_axis=0, tile...  50 us
    all_to_all x1, blocking collectives, local(): lax.all_to_all(partial_value.reshape(devices, CAP, model_width), ('dev',...  46.8 us
    dot_general x1, matrix products, local(): jnp.dot(combine.T, merged.reshape(window * CAP, model_width), precision=l...  4.27 us
    dot_general x1, matrix products, local(): jnp.dot(hidden, down_proj[0], preferred_element_type=jnp.float32)  3.58 us
    reshape x1, local copies, waits for them, and re-layouts, local(): partial_value.reshape(devices, CAP, model_width)  2.57 us

commit v1 on v0

--- a/solution.py
+++ b/solution.py
@@ -1,10 +1,320 @@
+import functools
+
 import jax
 import jax.numpy as jnp
 from jax import lax
+from jax.experimental import pallas as pl
+from jax.experimental.pallas import tpu as pltpu
 from jax.sharding import PartitionSpec as P
 
 SH = 16
 CAP = 6
+PARTS = 8
+ROWS = PARTS * CAP
+NZ = 4
+F32 = jnp.float32
+BF16 = jnp.bfloat16
+MESH = pl.DeviceIdType.MESH
+
+
+def iota(shape, dim):
+    return lax.broadcasted_iota(jnp.int32, shape, dim)
+
+
+def mm(a, b):
+    return jnp.dot(a, b, preferred_element_type=F32)
+
+
+def lane_plan(ids):
+    tok = ids.shape[0]
+    match = (ids == 0).astype(F32).astype(BF16)
+    ones = jnp.ones((ROWS, ids.shape[1]), BF16)
+    count = lax.dot_general(ones, match, (((1,), (1,)), ((), ())), preferred_element_type=F32)
+    upper = (iota((tok, tok), 0) <= iota((tok, tok), 1)).astype(F32).astype(BF16)
+    rank = mm(count.astype(BF16), upper)
+    return count > 0.5, (rank + 0.5).astype(jnp.int32) - 1
+
+
+def move_matrix(transposed):
+    big, small = PARTS * 32, NZ * ROWS
+    shape = (small, big) if transposed else (big, small)
+    a = iota(shape, 1 if transposed else 0)
+    b = iota(shape, 0 if transposed else 1)
+    p, j, r = a >> 5, (a >> 3) & 3, a & 7
+    return ((b == j * ROWS + p * CAP + r) & (r < CAP)).astype(F32).astype(BF16)
+
+
+def moe_kernel(ids_ref, tok_hbm, gate_hbm, up_hbm, down_hbm, out_ref,
+               tok, gu, dn, wire, xbuf, ybuf, part, sib_in, y_in, y_out, zu_in, zd_in, zu_out, zd_out,
+               loc, ag_recv, ag_up, ag_down, ag_y, ag_sib,
+               s_send, s_recv, y_send, y_recv, zu_send, zu_recv, zd_send, zd_recv):
+    width = wire.shape[2]
+    g, dev, c = lax.axis_index("groups"), lax.axis_index("dev"), lax.axis_index("sub")
+    z, y = dev // 2, dev % 2
+    up_dev, down_dev = (g, dev + 2, c), (g, dev - 2, c)
+    y_dev, sib_dev = (g, z * 2 + 1 - y, c), (g, dev, 1 - c)
+
+    barrier = pltpu.get_barrier_semaphore()
+
+    def greet(device):
+        pl.semaphore_signal(barrier, inc=1, device_id=device, device_id_type=MESH)
+
+    load_tok = pltpu.make_async_copy(tok_hbm, tok, loc.at[0])
+    load_gate = pltpu.make_async_copy(gate_hbm.at[0], gu.at[:, 0:128], loc.at[1])
+    load_up = pltpu.make_async_copy(up_hbm.at[0], gu.at[:, 128:256], loc.at[2])
+    load_down = pltpu.make_async_copy(down_hbm.at[0], dn, loc.at[3])
+    load_tok.start()
+    greet(sib_dev)
+    greet(y_dev)
+    pl.when(z < NZ - 1)(lambda: greet(up_dev))
+    pl.when(z > 0)(lambda: greet(down_dev))
+    load_gate.start()
+    load_up.start()
+    load_down.start()
+
+    def remote(src, dst, ss, rs, device):
+        return pltpu.make_async_remote_copy(
+            src_ref=src, dst_ref=dst, send_sem=ss, recv_sem=rs, device_id=device, device_id_type=MESH)
+
+    def slot(zz, yy, cc):
+        return zz * 4 + yy * 2 + cc
+
+    def gather(zz, yy, ss, device):
+        s = slot(zz, yy, c)
+        return remote(wire.at[s], wire.at[s], ss, ag_recv.at[s], device)
+
+    def to_up(zz):
+        return gather(zz, y, ag_up.at[zz], up_dev)
+
+    def to_down(zz):
+        return gather(zz, y, ag_down.at[zz], down_dev)
+
+    def to_y(zz):
+        return gather(zz, y, ag_y.at[zz], y_dev)
+
+    def to_sib(zz, yy):
+        return gather(zz, yy, ag_sib.at[zz * 2 + yy], sib_dev)
+
+    def arrived(zz, yy, cc):
+        s = slot(zz, yy, cc)
+        remote(wire.at[s], wire.at[s], ag_y.at[0], ag_recv.at[s], y_dev).wait_recv()
+
+    count, place = lane_plan(ids_ref[...])
+    row = iota(place.shape, 0)
+    load_tok.wait()
+    acc = jnp.zeros((ROWS, width), F32)
+    for p in range(PARTS):
+        r = row - p * CAP
+        sel = (count & (place == r) & (r >= 0) & (r < CAP)).astype(F32).astype(BF16)
+        acc += mm(sel, tok[:, p * width:(p + 1) * width])
+    wire[slot(z, y, c)] = acc.astype(BF16)
+
+    pl.semaphore_wait(barrier, 2 + (z + NZ - 2) // (NZ - 1) + (2 * NZ - 3 - z) // (NZ - 1))
+
+    pl.when(z < NZ - 1)(lambda: to_up(z).start())
+    pl.when(z > 0)(lambda: to_down(z).start())
+    to_y(z).start()
+    to_sib(z, y).start()
+
+    def relay_up(zz):
+        arrived(zz, y, c)
+        pl.when(z < NZ - 1)(lambda: to_up(zz).start())
+        to_y(zz).start()
+        to_sib(zz, y).start()
+
+    def relay_down(zz):
+        arrived(zz, y, c)
+        pl.when(z > 0)(lambda: to_down(zz).start())
+        to_y(zz).start()
+        to_sib(zz, y).start()
+
+    def relay_sib(zz):
+        arrived(zz, 1 - y, c)
+        to_sib(zz, 1 - y).start()
+
+    for d in range(1, NZ + 1):
+        if d < NZ:
+            pl.when(z - d >= 0)(functools.partial(relay_up, z - d))
+            pl.when(z + d < NZ)(functools.partial(relay_down, z + d))
+        if d == 1:
+            relay_sib(z)
+        else:
+            pl.when(z - (d - 1) >= 0)(functools.partial(relay_sib, z - (d - 1)))
+            pl.when(z + (d - 1) < NZ)(functools.partial(relay_sib, z + (d - 1)))
+
+    half = z // 2
+    far = NZ - 1 - (NZ - 1) * half
+    mid = 2 - half
+    order = (far, mid, 6 - far - mid - z, z)
+
+    move = move_matrix(False)
+    for zz in order[::-1]:
+        arrived(zz, 0, 1 - c)
+        arrived(zz, 1, 1 - c)
+        rows = mm(move, wire[pl.ds(zz * 4, 4)].reshape(4 * ROWS, width)).astype(BF16)
+        for p in range(PARTS):
+            xbuf[pl.ds(pl.multiple_of(zz * 32, 32), 32), p * width:(p + 1) * width] = rows[p * 32:(p + 1) * 32]
+
+    load_gate.wait()
+    load_up.wait()
+    act = jnp.zeros((NZ * 32, 256), F32)
+    for p in range(PARTS):
+        act += mm(xbuf[:, p * width:(p + 1) * width], gu[p * width:(p + 1) * width, :])
+    gate, upv = act[:, :128], act[:, 128:]
+    hidden = (gate / (1.0 + jnp.exp(-gate)) * upv).astype(BF16)
+
+    load_down.wait()
+    for p in range(PARTS):
+        val = mm(hidden, dn[:, p * width:(p + 1) * width]).astype(BF16)
+        for zz in range(NZ):
+            ybuf[zz, p * 32:(p + 1) * 32] = val[zz * 32:(zz + 1) * 32]
+
+    def s_copy(zz, yy):
+        k = zz * 2 + yy
+        return remote(part.at[slot(zz, yy, 1 - c)], sib_in.at[k], s_send.at[k], s_recv.at[k], sib_dev)
+
+    def y_copy(zz):
+        return remote(y_out.at[zz], y_in.at[zz], y_send.at[zz], y_recv.at[zz], y_dev)
+
+    def zu_copy(zz):
+        return remote(zu_out.at[zz], zu_in.at[zz], zu_send.at[zz], zu_recv.at[zz], up_dev)
+
+    def zd_copy(zz):
+        return remote(zd_out.at[zz], zd_in.at[zz], zd_send.at[zz], zd_recv.at[zz], down_dev)
+
+    back = move_matrix(True)
+    for zz in order:
+        vals = mm(back, ybuf[zz]).astype(BF16)
+        part[pl.ds(zz * 4, 4)] = vals.reshape(4, ROWS, width)
+        s_copy(zz, 1 - y).start()
+        s_copy(zz, y).start()
+
+    for zz in order:
+        s_copy(zz, 1 - y).wait_recv()
+        y_out[zz] = (part[slot(zz, 1 - y, c)].astype(F32) + sib_in[zz * 2 + 1 - y].astype(F32)).astype(BF16)
+        y_copy(zz).start()
+
+    def mine(zz):
+        s_copy(zz, y).wait_recv()
+        y_copy(zz).wait_recv()
+        return part[slot(zz, y, c)].astype(F32) + sib_in[zz * 2 + y].astype(F32) + y_in[zz].astype(F32)
+
+    def send_up(zz):
+        zu_out[zz] = mine(zz).astype(BF16)
+
+        @pl.when(z > 0)
+        def _():
+            zu_copy(zz).wait_recv()
+            zu_out[zz] = (zu_out[zz].astype(F32) + zu_in[zz].astype(F32)).astype(BF16)
+
+        zu_copy(zz).start()
+
+    def send_down(zz):
+        zd_out[zz] = mine(zz).astype(BF16)
+
+        @pl.when(z < NZ - 1)
+        def _():
+            zd_copy(zz).wait_recv()
+            zd_out[zz] = (zd_out[zz].astype(F32) + zd_in[zz].astype(F32)).astype(BF16)
+
+        zd_copy(zz).start()
+
+    for d in range(NZ - 1, 0, -1):
+        pl.when(z + d < NZ)(functools.partial(send_up, z + d))
+        pl.when(z - d >= 0)(functools.partial(send_down, z - d))
+    out_ref[...] = mine(z)
+
+    @pl.when(z > 0)
+    def _():
+        zu_copy(z).wait_recv()
+        out_ref[...] += zu_in[z].astype(F32)
+
+    @pl.when(z < NZ - 1)
+    def _():
+        zd_copy(z).wait_recv()
+        out_ref[...] += zd_in[z].astype(F32)
+
+    for zz in range(NZ):
+        pl.when((z < NZ - 1) & (zz <= z))(functools.partial(lambda k: to_up(k).wait_send(), zz))
+        pl.when((z > 0) & (zz >= z))(functools.partial(lambda k: to_down(k).wait_send(), zz))
+        to_y(zz).wait_send()
+        y_copy(zz).wait_send()
+        for yy in range(2):
+            to_sib(zz, yy).wait_send()
+            s_copy(zz, yy).wait_send()
+        pl.when(zz > z)(functools.partial(lambda k: zu_copy(k).wait_send(), zz))
+        pl.when(zz < z)(functools.partial(lambda k: zd_copy(k).wait_send(), zz))
+
+
+def spread_kernel(ids_ref, gates_ref, merged_ref, out_hbm, stage, sems):
+    ids = ids_ref[...]
+    tok, width = ids.shape[0], merged_ref.shape[1]
+    hit = ids == 0
+    match = hit.astype(F32)
+    weight = jnp.sum(jnp.where(hit, gates_ref[...], 0.0), axis=1, keepdims=True)
+    count = jnp.sum(match, axis=1, keepdims=True) > 0.5
+    lower = (iota((tok, tok), 0) >= iota((tok, tok), 1)).astype(F32).astype(BF16)
+    rank = jnp.sum(mm(lower, match.astype(BF16)), axis=1, keepdims=True)
+    place = (rank + 0.5).astype(jnp.int32) - 1
+    merged = merged_ref[...]
+    high = merged.astype(BF16)
+    rest = merged - high.astype(F32)
+    middle = rest.astype(BF16)
+    low = (rest - middle.astype(F32)).astype(BF16)
+    col = iota((tok, ROWS), 1)
+    copies = []
+    for p in range(PARTS):
+        r = col - p * CAP
+        sel = (count & (place == r) & (r >= 0) & (r < CAP)).astype(F32).astype(BF16)
+        val = (mm(sel, high) + mm(sel, middle)) + mm(sel, low)
+        stage[:, p * width:(p + 1) * width] = (val * weight).astype(BF16)
+        cols = pl.ds(p * width, width)
+        copy = pltpu.make_async_copy(stage.at[:, cols], out_hbm.at[:, cols], sems.at[p])
+        copy.start()
+        copies.append(copy)
+    for copy in copies:
+        copy.wait()
+
+
+def fast(tokens, expert_ids, gate_values, gate_proj, up_proj, down_proj):
+    tok, model = tokens.shape
+    width = model // PARTS
+    vmem = pl.BlockSpec(memory_space=pltpu.VMEM)
+    hbm = pl.BlockSpec(memory_space=pl.ANY)
+    dma = pltpu.SemaphoreType.DMA
+
+    def blocks(n):
+        return pltpu.VMEM((n, ROWS, width), BF16)
+
+    merged = pl.pallas_call(
+        moe_kernel,
+        out_shape=jax.ShapeDtypeStruct((ROWS, width), F32),
+        in_specs=[vmem, hbm, hbm, hbm, hbm],
+        out_specs=vmem,
+        scratch_shapes=[
+            pltpu.VMEM((tok, model), BF16),
+            pltpu.VMEM((model, 256), BF16),
+            pltpu.VMEM((128, model), BF16),
+            blocks(SH),
+            pltpu.VMEM((NZ * 32, model), BF16),
+            pltpu.VMEM((NZ, PARTS * 32, width), BF16),
+            blocks(SH), blocks(8), blocks(NZ), blocks(NZ), blocks(NZ), blocks(NZ), blocks(NZ), blocks(NZ),
+            dma((4,)), dma((SH,)), dma((NZ,)), dma((NZ,)), dma((NZ,)), dma((8,)),
+            dma((8,)), dma((8,)), dma((NZ,)), dma((NZ,)), dma((NZ,)), dma((NZ,)), dma((NZ,)), dma((NZ,)),
+        ],
+        compiler_params=pltpu.CompilerParams(
+            collective_id=0, has_side_effects=True, vmem_limit_bytes=48 * 1024 * 1024),
+        name="expert",
+    )(expert_ids, tokens, gate_proj, up_proj, down_proj)
+    return pl.pallas_call(
+        spread_kernel,
+        out_shape=jax.ShapeDtypeStruct((tok, model), BF16),
+        in_specs=[vmem, vmem, vmem],
+        out_specs=hbm,
+        scratch_shapes=[pltpu.VMEM((tok, model), BF16), dma((PARTS,))],
+        compiler_params=pltpu.CompilerParams(vmem_limit_bytes=32 * 1024 * 1024),
+        name="spread",
+    )(expert_ids, gate_values, merged)
 
 
 def plan(expert_ids, gate_values, window):
@@ -20,7 +330,7 @@
     return (chosen, weight)
 
 
-def local(tokens, expert_ids, gate_values, gate_proj, up_proj, down_proj):
+def general(tokens, expert_ids, gate_values, gate_proj, up_proj, down_proj):
     devices = lax.axis_size("dev") * lax.axis_size("sub")
     window = devices // SH
     model_width = tokens.shape[1]
@@ -68,8 +378,9 @@
         P(("dev", "sub"), None, None),
         P(("dev", "sub"), None, None),
     )
+    one_expert = mesh.shape["dev"] == 2 * NZ and mesh.shape["sub"] == 2
     return jax.shard_map(
-        local,
+        fast if one_expert else general,
         mesh=mesh,
         in_specs=placed,
         out_specs=P(("groups", "dev", "sub"), None),

time: 115 us -> 47.3 us (0.41)
  blocking collectives: 96.8 us -> 0 us
  Pallas kernels: 0 us -> 41 us
  matrix products: 11.7 us -> 0 us
  other arithmetic: 1.53 us -> 0 us
  local copies, waits for them, and re-layouts: 4.59 us -> 6.07 us
    all_to_all x2 -> x0, blocking collectives: 96.8 us -> none  [the longest x1 50 us: local(): lax.all_to_all(sendbuf, ('dev', 'sub'), split_axis=0, concat_axis=0, tile...]
    pallas_call x0 -> x2, Pallas kernels: none -> 41 us  [the longest x1 38.3 us: fast(): pl.pallas_call(moe_kernel, out_shape=jax.ShapeDtypeStruct((ROWS, width),...]
    dot_general x4 -> x0, matrix products: 11.7 us -> none  [the longest x1 4.27 us: local(): jnp.dot(combine.T, merged.reshape(window * CAP, model_width), precision=l...]
    unnamed x2 -> x8, local copies, waits for them, and re-layouts: 0.01 us -> 6.07 us
    reshape x3 -> x0, local copies, waits for them, and re-layouts: 4.47 us -> none  [the longest x1 2.57 us: local(): partial_value.reshape(devices, CAP, model_width)]
    reduce_sum x3 -> x0, other arithmetic: 1.25 us -> none  [the longest x1 0.85 us: plan(): jnp.sum(jnp.where(matches, gate_values[:, :, None], jnp.zeros_like(gate_v...]
where the time goes in v1:
time: 47.3 us; the launch traced here: 47.1 us
  Pallas kernels  41 us (87%)
  local copies, waits for them, and re-layouts  6.07 us (13%)
    pallas_call x1, Pallas kernels, fast(): pl.pallas_call(moe_kernel, out_shape=jax.ShapeDtypeStruct((ROWS, width),...  38.3 us
    unnamed x8, local copies, waits for them, and re-layouts  6.07 us
    pallas_call x1, Pallas kernels, fast(): pl.pallas_call(spread_kernel, out_shape=jax.ShapeDtypeStruct((tok, model)...  2.64 us

profile of v1, /device:TPU:0, one launch (start us, length us, event | category | flops | bytes accessed | tf_op | source)
XLA Modules:
  0.0 47.1 jit_solution(7812307030981201496)
XLA Ops:
  0.0 0.8 %copy.8.ids_ref = s32[128,8]{1,0:T(8,128)S(1)} copy(s32[128,8]{0,1:T(8,128)} %param.7) | data formatting | bytes 8192 | tf_op args[1]
  0.8 0.8 %copy.9.gates_ref = f32[128,8]{1,0:T(8,128)S(1)} copy(f32[128,8]{0,1:T(8,128)} %param.8) | data formatting | bytes 8192 | tf_op args[2]
  1.6 0.0 copy-start
  1.6 1.5 %copy-done = bf16[128,7168]{1,0:T(8,128)(2,1)S(1)} copy-done((bf16[128,7168]{1,0:T(8,128)(2,1)S(1)}, bf16[128,7168]{1,0:T(8,128)(2,1)}, u32[]{:S(2)}) %copy-start) | copy-done | bytes 1835032
  3.1 0.0 copy-start.1
  3.1 1.5 %copy-done.1 = bf16[1,7168,128]{2,1,0:T(8,128)(2,1)S(1)} copy-done((bf16[1,7168,128]{2,1,0:T(8,128)(2,1)S(1)}, bf16[1,7168,128]{2,1,0:T(8,128)(2,1)}, u32[]{:S(2)}) %copy-start.1) | copy-done | bytes 1835032
  4.6 0.0 copy-start.2
  4.6 1.5 %copy-done.2 = bf16[1,7168,128]{2,1,0:T(8,128)(2,1)S(1)} copy-done((bf16[1,7168,128]{2,1,0:T(8,128)(2,1)S(1)}, bf16[1,7168,128]{2,1,0:T(8,128)(2,1)}, u32[]{:S(2)}) %copy-start.2) | copy-done | bytes 1835032
  6.1 38.3 %expert.1.merged_ref = f32[48,896]{1,0:T(8,128)S(1)} custom-call(s32[128,8]{1,0:T(8,128)S(1)} %copy.8.ids_ref, bf16[128,7168]{1,0:T(8,128)(2,1)S(1)} %copy-done, bf16[1,7168,128]{2,1,0:T(8,128)(2,1)S(1)} %copy-done.1, bf16[1,7168,128]{2,1,0:T(8,128)(2,1)S(1)} %copy-done.2, bf16[1,128,7168]{2,1,0:T(8,128)(2,1)} %down_hbm.1), custom_call_target="tpu_custom_call" | custom-call | tf_op jit(solution)/shard_map/expert/pallas_call | solution.py:289
  44.4 2.6 %spread.1 = bf16[128,7168]{1,0:T(8,128)(2,1)} custom-call(s32[128,8]{1,0:T(8,128)S(1)} %copy.8.ids_ref, f32[128,8]{1,0:T(8,128)S(1)} %copy.9.gates_ref, f32[48,896]{1,0:T(8,128)S(1)} %expert.1.merged_ref), custom_call_target="tpu_custom_call" | custom-call | tf_op jit(solution)/shard_map/spread/pallas_call | solution.py:309
Async XLA Ops:
  1.6 1.5 %copy-start = (bf16[128,7168]{1,0:T(8,128)(2,1)S(1)}, bf16[128,7168]{1,0:T(8,128)(2,1)}, u32[]{:S(2)}) copy-start(bf16[128,7168]{1,0:T(8,128)(2,1)} %tok_hbm.1) | copy-start | bytes 5505028
  3.1 1.5 %copy-start.1 = (bf16[1,7168,128]{2,1,0:T(8,128)(2,1)S(1)}, bf16[1,7168,128]{2,1,0:T(8,128)(2,1)}, u32[]{:S(2)}) copy-start(bf16[1,7168,128]{2,1,0:T(8,128)(2,1)} %gate_hbm.1) | copy-start | bytes 5505028
  4.6 1.5 %copy-start.2 = (bf16[1,7168,128]{2,1,0:T(8,128)(2,1)S(1)}, bf16[1,7168,128]{2,1,0:T(8,128)(2,1)}, u32[]{:S(2)}) copy-start(bf16[1,7168,128]{2,1,0:T(8,128)(2,1)} %up_hbm.1) | copy-start | bytes 5505028

commit v2 on v1

v2 whole, which is shorter than its diff:
```python
import functools

import jax
import jax.numpy as jnp
from jax import lax
from jax.experimental import pallas as pl
from jax.experimental.pallas import tpu as pltpu
from jax.sharding import PartitionSpec as P

SH = 16
CAP = 6
PARTS = 8
ROWS = PARTS * CAP
NZ = 4
NC = 3
PIECE = ROWS // NC
F32 = jnp.float32
BF16 = jnp.bfloat16
MESH = pl.DeviceIdType.MESH


def iota(shape, dim):
    return lax.broadcasted_iota(jnp.int32, shape, dim)


def mm(a, b):
    return jnp.dot(a, b, preferred_element_type=F32)


def lane_plan(ids):
    tok = ids.shape[1]
    match = (ids == 0).astype(F32).astype(BF16)
    count = mm(jnp.ones((ROWS, ids.shape[0]), BF16), match)
    upper = (iota((tok, tok), 0) <= iota((tok, tok), 1)).astype(F32).astype(BF16)
    rank = mm(count.astype(BF16), upper)
    return count > 0.5, (rank + 0.5).astype(jnp.int32) - 1


def move_matrix(transposed):
    big, small = PARTS * 32, NZ * ROWS
    shape = (small, big) if transposed else (big, small)
    a = iota(shape, 1 if transposed else 0)
    b = iota(shape, 0 if transposed else 1)
    p, j, r = a >> 5, (a >> 3) & 3, a & 7
    return ((b == j * ROWS + p * CAP + r) & (r < CAP)).astype(F32).astype(BF16)


def moe_kernel(ids_hbm, gates_hbm, tok_hbm, gate_hbm, up_hbm, down_hbm, out_ref, place_ref, weight_ref,
               ids_v, gates_v, tok, gu, dn, wire, xbuf, ybuf, part, sib_in, y_in, y_out, zu_in, zd_in, zu_out, zd_out,
               loc, ag_recv, ag_up, ag_down, ag_y, ag_sib,
               s_send, s_recv, y_send, y_recv, zu_send, zu_recv, zd_send, zd_recv):
    width = wire.shape[2]
    g, dev, c = lax.axis_index("groups"), lax.axis_index("dev"), lax.axis_index("sub")
    z, y = dev // 2, dev % 2
    up_dev, down_dev = (g, dev + 2, c), (g, dev - 2, c)
    y_dev, sib_dev = (g, z * 2 + 1 - y, c), (g, dev, 1 - c)

    barrier = pltpu.get_barrier_semaphore()

    def greet(device):
        pl.semaphore_signal(barrier, inc=1, device_id=device, device_id_type=MESH)

    load_tok = pltpu.make_async_copy(tok_hbm, tok, loc.at[0])
    load_gate = pltpu.make_async_copy(gate_hbm.at[0], gu.at[:, 0:128], loc.at[1])
    load_up = pltpu.make_async_copy(up_hbm.at[0], gu.at[:, 128:256], loc.at[2])
    load_down = pltpu.make_async_copy(down_hbm.at[0], dn, loc.at[3])
    load_ids = pltpu.make_async_copy(ids_hbm, ids_v, loc.at[4])
    load_gates = pltpu.make_async_copy(gates_hbm, gates_v, loc.at[5])
    load_ids.start()
    load_tok.start()
    load_gates.start()
    greet(sib_dev)
    greet(y_dev)
    pl.when(z < NZ - 1)(lambda: greet(up_dev))
    pl.when(z > 0)(lambda: greet(down_dev))
    load_gate.start()
    load_up.start()
    load_down.start()

    def remote(src, dst, ss, rs, device):
        return pltpu.make_async_remote_copy(
            src_ref=src, dst_ref=dst, send_sem=ss, recv_sem=rs, device_id=device, device_id_type=MESH)

    def slot(zz, yy, cc):
        return zz * 4 + yy * 2 + cc

    def gather(zz, yy, k, ss, device):
        piece = wire.at[slot(zz, yy, c), pl.ds(k * PIECE, PIECE)]
        return remote(piece, piece, ss, ag_recv.at[slot(zz, yy, c) * NC + k], device)

    def to_up(zz, k):
        return gather(zz, y, k, ag_up.at[zz * NC + k], up_dev)

    def to_down(zz, k):
        return gather(zz, y, k, ag_down.at[zz * NC + k], down_dev)

    def to_y(zz, k):
        return gather(zz, y, k, ag_y.at[zz * NC + k], y_dev)

    def to_sib(zz, yy, k):
        return gather(zz, yy, k, ag_sib.at[(zz * 2 + yy) * NC + k], sib_dev)

    def arrived(zz, yy, cc, k):
        piece = wire.at[slot(zz, yy, cc), pl.ds(k * PIECE, PIECE)]
        remote(piece, piece, ag_y.at[0], ag_recv.at[slot(zz, yy, cc) * NC + k], y_dev).wait_recv()

    load_ids.wait()
    count, place = lane_plan(ids_v[...])
    row = iota(place.shape, 0)
    load_tok.wait()
    acc = jnp.zeros((ROWS, width), F32)
    for p in range(PARTS):
        r = row - p * CAP
        sel = (count & (place == r) & (r >= 0) & (r < CAP)).astype(F32).astype(BF16)
        acc += mm(sel, tok[:, p * width:(p + 1) * width])
    wire[slot(z, y, c)] = acc.astype(BF16)

    pl.semaphore_wait(barrier, 2 + (z + NZ - 2) // (NZ - 1) + (2 * NZ - 3 - z) // (NZ - 1))

    def first_up(k):
        pl.when(z < NZ - 1)(lambda: to_up(z, k).start())

    def first_down(k):
        pl.when(z > 0)(lambda: to_down(z, k).start())

    for k in range(NC):
        first_up(k)
        first_down(k)
        to_y(z, k).start()
    for k in range(NC):
        to_sib(z, y, k).start()

    def relay_up(zz, k):
        arrived(zz, y, c, k)
        pl.when(z < NZ - 1)(lambda: to_up(zz, k).start())
        to_y(zz, k).start()
        to_sib(zz, y, k).start()

    def relay_down(zz, k):
        arrived(zz, y, c, k)
        pl.when(z > 0)(lambda: to_down(zz, k).start())
        to_y(zz, k).start()
        to_sib(zz, y, k).start()

    def relay_sib(zz, k):
        arrived(zz, 1 - y, c, k)
        to_sib(zz, 1 - y, k).start()

    load_gates.wait()
    ids, gate_cols = ids_v[...].T, gates_v[...].T
    tokens = ids.shape[0]
    hit = ids == 0
    match = hit.astype(F32)
    weight = jnp.sum(jnp.where(hit, gate_cols, 0.0), axis=1, keepdims=True)
    named = jnp.sum(match, axis=1, keepdims=True) > 0.5
    lower = (iota((tokens, tokens), 0) >= iota((tokens, tokens), 1)).astype(F32).astype(BF16)
    rank = jnp.sum(mm(lower, match.astype(BF16)), axis=1, keepdims=True)
    taken = (rank + 0.5).astype(jnp.int32) - 1
    taken = jnp.where(named & (taken < CAP), taken, -ROWS)
    place_ref[...] = jnp.broadcast_to(taken, place_ref.shape)
    weight_ref[...] = jnp.broadcast_to(weight, weight_ref.shape)

    for d in range(1, NZ + 1):
        for k in range(NC):
            if d < NZ:
                pl.when(z - d >= 0)(functools.partial(relay_up, z - d, k))
                pl.when(z + d < NZ)(functools.partial(relay_down, z + d, k))
            if d == 1:
                relay_sib(z, k)
            else:
                pl.when(z - (d - 1) >= 0)(functools.partial(relay_sib, z - (d - 1), k))
                pl.when(z + (d - 1) < NZ)(functools.partial(relay_sib, z + (d - 1), k))

    half = z // 2
    far = NZ - 1 - (NZ - 1) * half
    mid = 2 - half
    order = (far, mid, 6 - far - mid - z, z)

    move = move_matrix(False)
    for zz in order[::-1]:
        for k in range(NC):
            arrived(zz, 0, 1 - c, k)
            arrived(zz, 1, 1 - c, k)
        rows = mm(move, wire[pl.ds(zz * 4, 4)].reshape(4 * ROWS, width)).astype(BF16)
        for p in range(PARTS):
            xbuf[pl.ds(pl.multiple_of(zz * 32, 32), 32), p * width:(p + 1) * width] = rows[p * 32:(p + 1) * 32]

    load_gate.wait()
    load_up.wait()
    act = jnp.zeros((NZ * 32, 256), F32)
    for p in range(PARTS):
        act += mm(xbuf[:, p * width:(p + 1) * width], gu[p * width:(p + 1) * width, :])
    gate, upv = act[:, :128], act[:, 128:]
    hidden = (gate / (1.0 + jnp.exp(-gate)) * upv).astype(BF16)

    load_down.wait()
    for p in range(PARTS):
        val = mm(hidden, dn[:, p * width:(p + 1) * width]).astype(BF16)
        for zz in range(NZ):
            ybuf[zz, p * 32:(p + 1) * 32] = val[zz * 32:(zz + 1) * 32]

    def rows_of(k):
        return pl.ds(k * PIECE, PIECE)

    def s_copy(zz, yy, k):
        n = (zz * 2 + yy) * NC + k
        return remote(part.at[slot(zz, yy, 1 - c), rows_of(k)], sib_in.at[zz * 2 + yy, rows_of(k)],
                      s_send.at[n], s_recv.at[n], sib_dev)

    def line(src, dst, ss, rs, device):
        def copy(zz, k):
            n = zz * NC + k
            return remote(src.at[zz, rows_of(k)], dst.at[zz, rows_of(k)], ss.at[n], rs.at[n], device)
        return copy

    y_copy = line(y_out, y_in, y_send, y_recv, y_dev)
    zu_copy = line(zu_out, zu_in, zu_send, zu_recv, up_dev)
    zd_copy = line(zd_out, zd_in, zd_send, zd_recv, down_dev)

    back = move_matrix(True)
    for zz in order:
        vals = mm(back, ybuf[zz]).astype(BF16)
        part[pl.ds(zz * 4, 4)] = vals.reshape(4, ROWS, width)
        for yy in (1 - y, y):
            for k in range(NC):
                s_copy(zz, yy, k).start()

    for zz in order:
        for k in range(NC):
            s_copy(zz, 1 - y, k).wait_recv()
            at = rows_of(k)
            y_out[zz, at] = (part[slot(zz, 1 - y, c), at].astype(F32) + sib_in[zz * 2 + 1 - y, at].astype(F32)).astype(BF16)
            y_copy(zz, k).start()

    def mine(zz, k):
        s_copy(zz, y, k).wait_recv()
        y_copy(zz, k).wait_recv()
        at = rows_of(k)
        return part[slot(zz, y, c), at].astype(F32) + sib_in[zz * 2 + y, at].astype(F32) + y_in[zz, at].astype(F32)

    def send_line(copy, out, inn, inner, zz, k):
        at = rows_of(k)
        out[zz, at] = mine(zz, k).astype(BF16)

        @pl.when(inner)
        def _():
            copy(zz, k).wait_recv()
            out[zz, at] = (mine_again(zz, k) + inn[zz, at].astype(F32)).astype(BF16)

        copy(zz, k).start()

    def mine_again(zz, k):
        at = rows_of(k)
        return part[slot(zz, y, c), at].astype(F32) + sib_in[zz * 2 + y, at].astype(F32) + y_in[zz, at].astype(F32)

    for d in range(NZ - 1, 0, -1):
        for k in range(NC):
            pl.when(z + d < NZ)(functools.partial(send_line, zu_copy, zu_out, zu_in, z > 0, z + d, k))
            pl.when(z - d >= 0)(functools.partial(send_line, zd_copy, zd_out, zd_in, z < NZ - 1, z - d, k))
    for k in range(NC):
        out_ref[rows_of(k)] = mine(z, k)

    @pl.when(z > 0)
    def _():
        for k in range(NC):
            zu_copy(z, k).wait_recv()
            out_ref[rows_of(k)] += zu_in[z, rows_of(k)].astype(F32)

    @pl.when(z < NZ - 1)
    def _():
        for k in range(NC):
            zd_copy(z, k).wait_recv()
            out_ref[rows_of(k)] += zd_in[z, rows_of(k)].astype(F32)

    def left(copy, zz, k):
        copy(zz, k).wait_send()

    for zz in range(NZ):
        for k in range(NC):
            pl.when((z < NZ - 1) & (zz <= z))(functools.partial(left, to_up, zz, k))
            pl.when((z > 0) & (zz >= z))(functools.partial(left, to_down, zz, k))
            to_y(zz, k).wait_send()
            y_copy(zz, k).wait_send()
            for yy in range(2):
                to_sib(zz, yy, k).wait_send()
                s_copy(zz, yy, k).wait_send()
            pl.when(zz > z)(functools.partial(left, zu_copy, zz, k))
            pl.when(zz < z)(functools.partial(left, zd_copy, zz, k))


def spread_kernel(place_ref, weight_ref, merged_ref, out_hbm, stage, sems):
    tok, width = place_ref.shape[0], merged_ref.shape[1]
    place, weight = place_ref[:, :ROWS], weight_ref[:, :1]
    merged = merged_ref[...]
    high = merged.astype(BF16)
    rest = merged - high.astype(F32)
    middle = rest.astype(BF16)
    low = (rest - middle.astype(F32)).astype(BF16)
    col = iota((tok, ROWS), 1)
    copies = []
    for p in range(PARTS):
        sel = (place == col - p * CAP).astype(F32).astype(BF16)
        val = (mm(sel, high) + mm(sel, middle)) + mm(sel, low)
        stage[:, p * width:(p + 1) * width] = (val * weight).astype(BF16)
        cols = pl.ds(p * width, width)
        copy = pltpu.make_async_copy(stage.at[:, cols], out_hbm.at[:, cols], sems.at[p])
        copy.start()
        copies.append(copy)
    for copy in copies:
        copy.wait()


def fast(tokens, expert_ids, gate_values, gate_proj, up_proj, down_proj):
    tok, model = tokens.shape
    width = model // PARTS
    ids, gates = expert_ids.T, gate_values.T
    vmem = pl.BlockSpec(memory_space=pltpu.VMEM)
    hbm = pl.BlockSpec(memory_space=pltpu.HBM)
    dma = pltpu.SemaphoreType.DMA

    def blocks(n):
        return pltpu.VMEM((n, ROWS, width), BF16)

    merged, place, weight = pl.pallas_call(
        moe_kernel,
        out_shape=(jax.ShapeDtypeStruct((ROWS, width), F32), jax.ShapeDtypeStruct((tok, 128), jnp.int32),
                   jax.ShapeDtypeStruct((tok, 128), F32)),
        in_specs=[hbm] * 6,
        out_specs=(vmem, vmem, vmem),
        scratch_shapes=[
            pltpu.VMEM(ids.shape, jnp.int32),
            pltpu.VMEM(gates.shape, F32),
            pltpu.VMEM((tok, model), BF16),
            pltpu.VMEM((model, 256), BF16),
            pltpu.VMEM((128, model), BF16),
            blocks(SH),
            pltpu.VMEM((NZ * 32, model), BF16),
            pltpu.VMEM((NZ, PARTS * 32, width), BF16),
            blocks(SH), blocks(8), blocks(NZ), blocks(NZ), blocks(NZ), blocks(NZ), blocks(NZ), blocks(NZ),
            dma((6,)), dma((SH * NC,)), dma((NZ * NC,)), dma((NZ * NC,)), dma((NZ * NC,)), dma((8 * NC,)),
            dma((8 * NC,)), dma((8 * NC,)), dma((NZ * NC,)), dma((NZ * NC,)),
            dma((NZ * NC,)), dma((NZ * NC,)), dma((NZ * NC,)), dma((NZ * NC,)),
        ],
        compiler_params=pltpu.CompilerParams(
            collective_id=0, has_side_effects=True, vmem_limit_bytes=60 * 1024 * 1024),
        name="expert",
    )(ids, gates, tokens, gate_proj, up_proj, down_proj)
    return pl.pallas_call(
        spread_kernel,
        out_shape=jax.ShapeDtypeStruct((tok, model), BF16),
        in_specs=[vmem, vmem, vmem],
        out_specs=hbm,
        scratch_shapes=[pltpu.VMEM((tok, model), BF16), dma((PARTS,))],
        compiler_params=pltpu.CompilerParams(vmem_limit_bytes=32 * 1024 * 1024),
        name="spread",
    )(place, weight, merged)


def plan(expert_ids, gate_values, window):
    experts = jnp.arange(window, dtype=jnp.int32)
    matches = expert_ids[:, :, None] == experts[None, None, :]
    counts = jnp.sum(matches.astype(jnp.int32), axis=1)
    weight = jnp.sum(
        jnp.where(matches, gate_values[:, :, None], jnp.zeros_like(gate_values[:, :, None])), axis=1
    )
    ranking = jnp.cumsum(counts, axis=0) - 1
    slot_ids = jnp.arange(CAP, dtype=jnp.int32)
    chosen = (counts.T[:, None, :] == 1) & (ranking.T[:, None, :] == slot_ids[None, :, None])
    return (chosen, weight)


def general(tokens, expert_ids, gate_values, gate_proj, up_proj, down_proj):
    devices = lax.axis_size("dev") * lax.axis_size("sub")
    window = devices // SH
    model_width = tokens.shape[1]
    chosen, weight = plan(expert_ids, gate_values, window)
    picked = chosen.astype(jnp.bfloat16).reshape(window * CAP, tokens.shape[0])
    outbound = jnp.dot(picked, tokens, preferred_element_type=jnp.float32).astype(jnp.bfloat16)
    outbound = outbound.reshape(window, 1, CAP, model_width)
    sendbuf = jnp.broadcast_to(outbound, (window, SH, CAP, model_width)).reshape(
        devices, CAP, model_width
    )
    arrived = lax.all_to_all(sendbuf, ("dev", "sub"), split_axis=0, concat_axis=0, tiled=True)
    row_block = arrived.reshape(devices * CAP, model_width)
    gate_act = jnp.dot(row_block, gate_proj[0], preferred_element_type=jnp.float32)
    up_act = jnp.dot(row_block, up_proj[0], preferred_element_type=jnp.float32)
    hidden = (jax.nn.silu(gate_act) * up_act).astype(jnp.bfloat16)
    partial_value = jnp.dot(hidden, down_proj[0], preferred_element_type=jnp.float32).astype(
        jnp.bfloat16
    )
    returned = lax.all_to_all(
        partial_value.reshape(devices, CAP, model_width),
        ("dev", "sub"),
        split_axis=0,
        concat_axis=0,
        tiled=True,
    )
    merged = jnp.sum(returned.reshape(window, SH, CAP, model_width).astype(jnp.float32), axis=1)
    combine = (chosen.astype(jnp.float32) * weight.T[:, None, :]).reshape(
        window * CAP, tokens.shape[0]
    )
    moe_out = jnp.dot(
        combine.T,
        merged.reshape(window * CAP, model_width),
        precision=lax.Precision.HIGHEST,
        preferred_element_type=jnp.float32,
    )
    return moe_out.astype(jnp.bfloat16)


def solution(mesh):
    placed = (
        P(("groups", "dev", "sub"), None),
        P(("groups", "dev", "sub"), None),
        P(("groups", "dev", "sub"), None),
        P(("dev", "sub"), None, None),
        P(("dev", "sub"), None, None),
        P(("dev", "sub"), None, None),
    )
    one_expert = mesh.shape["dev"] == 2 * NZ and mesh.shape["sub"] == 2
    return jax.shard_map(
        fast if one_expert else general,
        mesh=mesh,
        in_specs=placed,
        out_specs=P(("groups", "dev", "sub"), None),
        check_vma=False,
    )
```

time: 47.3 us -> 45.3 us (0.958)
  local copies, waits for them, and re-layouts: 6.07 us -> 2.59 us
  Pallas kernels: 41 us -> 42.5 us
    unnamed x8 -> x6, local copies, waits for them, and re-layouts: 6.07 us -> 2.59 us
    pallas_call x1, Pallas kernels: 38.3 us -> 40 us  [fast(): pl.pallas_call(moe_kernel, out_shape=(jax.ShapeDtypeStruct((ROWS, width),...]
where the time goes in v2:
time: 45.3 us; the launch traced here: 45.1 us
  Pallas kernels  42.5 us (94%)
  local copies, waits for them, and re-layouts  2.59 us (6%)
    pallas_call x1, Pallas kernels, fast(): pl.pallas_call(moe_kernel, out_shape=(jax.ShapeDtypeStruct((ROWS, width),...  40 us
    unnamed x6, local copies, waits for them, and re-layouts  2.59 us
    pallas_call x1, Pallas kernels, fast(): pl.pallas_call(spread_kernel, out_shape=jax.ShapeDtypeStruct((tok, model)...  2.47 us

profile of v2, /device:TPU:0, one launch (start us, length us, event | category | flops | bytes accessed | tf_op | source)
XLA Modules:
  0.0 45.1 jit_solution(918279541172561744)
XLA Ops:
  0.0 40.0 %expert.1 = (f32[48,896]{1,0:T(8,128)}, s32[128,128]{1,0:T(8,128)}, f32[128,128]{1,0:T(8,128)}) custom-call(s32[8,128]{1,0:T(8,128)} %bitcast.2, f32[8,128]{1,0:T(8,128)} %bitcast.3, bf16[128,7168]{1,0:T(8,128)(2,1)} %tok_hbm.1, bf16[1,7168,128]{2,1,0:T(8,128)(2,1)} %gate_hbm.1, bf16[1,7168,128]{2,1,0:T(8,128)(2,1)} %up_hbm.1, bf16[1,128,7168]{2,1,0:T(8,128)(2,1)} %down_hbm.1), custom_call_target="tpu_custom_call" | custom-call | tf_op jit(solution)/shard_map/expert/pallas_call | solution.py:324
  40.0 0.0 copy-start
  40.0 0.9 %copy-done = f32[48,896]{1,0:T(8,128)S(1)} copy-done((f32[48,896]{1,0:T(8,128)S(1)}, f32[48,896]{1,0:T(8,128)}, u32[]{:S(2)}) %copy-start) | copy-done | bytes 172056
  40.9 0.0 copy-start.1
  40.9 0.8 %copy-done.1 = s32[128,128]{1,0:T(8,128)S(1)} copy-done((s32[128,128]{1,0:T(8,128)S(1)}, s32[128,128]{1,0:T(8,128)}, u32[]{:S(2)}) %copy-start.1) | copy-done | bytes 65560
  41.8 0.0 copy-start.2
  41.8 0.8 %copy-done.2 = f32[128,128]{1,0:T(8,128)S(1)} copy-done((f32[128,128]{1,0:T(8,128)S(1)}, f32[128,128]{1,0:T(8,128)}, u32[]{:S(2)}) %copy-start.2) | copy-done | bytes 65560
  42.6 2.5 %spread.1 = bf16[128,7168]{1,0:T(8,128)(2,1)} custom-call(s32[128,128]{1,0:T(8,128)S(1)} %copy-done.1, f32[128,128]{1,0:T(8,128)S(1)} %copy-done.2, f32[48,896]{1,0:T(8,128)S(1)} %copy-done), custom_call_target="tpu_custom_call" | custom-call | tf_op jit(solution)/shard_map/spread/pallas_call | solution.py:348
Async XLA Ops:
  40.0 0.9 %copy-start = (f32[48,896]{1,0:T(8,128)S(1)}, f32[48,896]{1,0:T(8,128)}, u32[]{:S(2)}) copy-start(f32[48,896]{1,0:T(8,128)} %get-tuple-element.10.merged_ref) | copy-start | bytes 516100
  40.9 0.8 %copy-start.1 = (s32[128,128]{1,0:T(8,128)S(1)}, s32[128,128]{1,0:T(8,128)}, u32[]{:S(2)}) copy-start(s32[128,128]{1,0:T(8,128)} %get-tuple-element.8.place_ref) | copy-start | bytes 196612
  41.8 0.8 %copy-start.2 = (f32[128,128]{1,0:T(8,128)S(1)}, f32[128,128]{1,0:T(8,128)}, u32[]{:S(2)}) copy-start(f32[128,128]{1,0:T(8,128)} %get-tuple-element.9.weight_ref) | copy-start | bytes 196612

commit v3 on v2

--- a/solution.py
+++ b/solution.py
@@ -46,13 +46,13 @@
 
 
 def moe_kernel(ids_hbm, gates_hbm, tok_hbm, gate_hbm, up_hbm, down_hbm, out_ref, place_ref, weight_ref,
-               ids_v, gates_v, tok, gu, dn, wire, xbuf, ybuf, part, sib_in, y_in, y_out, zu_in, zd_in, zu_out, zd_out,
-               loc, ag_recv, ag_up, ag_down, ag_y, ag_sib,
-               s_send, s_recv, y_send, y_recv, zu_send, zu_recv, zd_send, zd_recv):
+               ids_v, gates_v, tok, gu, dn, wire, xbuf, ybuf, part, sib_in, y_in, y_out, z_in, z_out,
+               loc, ag_recv, ag_z, ag_y, ag_sib,
+               s_send, s_recv, y_send, y_recv, z_send, z_recv):
     width = wire.shape[2]
     g, dev, c = lax.axis_index("groups"), lax.axis_index("dev"), lax.axis_index("sub")
     z, y = dev // 2, dev % 2
-    up_dev, down_dev = (g, dev + 2, c), (g, dev - 2, c)
+    others = [(z + j) % NZ for j in (1, 3, 2)]
     y_dev, sib_dev = (g, z * 2 + 1 - y, c), (g, dev, 1 - c)
 
     barrier = pltpu.get_barrier_semaphore()
@@ -71,8 +71,8 @@
     load_gates.start()
     greet(sib_dev)
     greet(y_dev)
-    pl.when(z < NZ - 1)(lambda: greet(up_dev))
-    pl.when(z > 0)(lambda: greet(down_dev))
+    for zz in others:
+        greet((g, zz * 2 + y, c))
     load_gate.start()
     load_up.start()
     load_down.start()
@@ -88,11 +88,8 @@
         piece = wire.at[slot(zz, yy, c), pl.ds(k * PIECE, PIECE)]
         return remote(piece, piece, ss, ag_recv.at[slot(zz, yy, c) * NC + k], device)
 
-    def to_up(zz, k):
-        return gather(zz, y, k, ag_up.at[zz * NC + k], up_dev)
-
-    def to_down(zz, k):
-        return gather(zz, y, k, ag_down.at[zz * NC + k], down_dev)
+    def to_z(zz, k):
+        return gather(z, y, k, ag_z.at[zz * NC + k], (g, zz * 2 + y, c))
 
     def to_y(zz, k):
         return gather(zz, y, k, ag_y.at[zz * NC + k], y_dev)
@@ -115,30 +112,17 @@
         acc += mm(sel, tok[:, p * width:(p + 1) * width])
     wire[slot(z, y, c)] = acc.astype(BF16)
 
-    pl.semaphore_wait(barrier, 2 + (z + NZ - 2) // (NZ - 1) + (2 * NZ - 3 - z) // (NZ - 1))
-
-    def first_up(k):
-        pl.when(z < NZ - 1)(lambda: to_up(z, k).start())
-
-    def first_down(k):
-        pl.when(z > 0)(lambda: to_down(z, k).start())
-
-    for k in range(NC):
-        first_up(k)
-        first_down(k)
+    pl.semaphore_wait(barrier, NZ + 1)
+
+    for k in range(NC):
+        for zz in others:
+            to_z(zz, k).start()
         to_y(z, k).start()
     for k in range(NC):
         to_sib(z, y, k).start()
 
-    def relay_up(zz, k):
+    def relay_z(zz, k):
         arrived(zz, y, c, k)
-        pl.when(z < NZ - 1)(lambda: to_up(zz, k).start())
-        to_y(zz, k).start()
-        to_sib(zz, y, k).start()
-
-    def relay_down(zz, k):
-        arrived(zz, y, c, k)
-        pl.when(z > 0)(lambda: to_down(zz, k).start())
         to_y(zz, k).start()
         to_sib(zz, y, k).start()
 
@@ -160,16 +144,15 @@
     place_ref[...] = jnp.broadcast_to(taken, place_ref.shape)
     weight_ref[...] = jnp.broadcast_to(weight, weight_ref.shape)
 
-    for d in range(1, NZ + 1):
-        for k in range(NC):
-            if d < NZ:
-                pl.when(z - d >= 0)(functools.partial(relay_up, z - d, k))
-                pl.when(z + d < NZ)(functools.partial(relay_down, z + d, k))
-            if d == 1:
-                relay_sib(z, k)
-            else:
-                pl.when(z - (d - 1) >= 0)(functools.partial(relay_sib, z - (d - 1), k))
-                pl.when(z + (d - 1) < NZ)(functools.partial(relay_sib, z + (d - 1), k))
+    for k in range(NC):
+        for zz in others:
+            relay_z(zz, k)
+        relay_sib(z, k)
+        if k > 0:
+            for zz in others:
+                relay_sib(zz, k - 1)
+    for zz in others:
+        relay_sib(zz, NC - 1)
 
     half = z // 2
     far = NZ - 1 - (NZ - 1) * half
@@ -214,8 +197,14 @@
         return copy
 
     y_copy = line(y_out, y_in, y_send, y_recv, y_dev)
-    zu_copy = line(zu_out, zu_in, zu_send, zu_recv, up_dev)
-    zd_copy = line(zd_out, zd_in, zd_send, zd_recv, down_dev)
+
+    def z_copy(zz, k):
+        return remote(z_out.at[zz, rows_of(k)], z_in.at[z, rows_of(k)],
+                      z_send.at[zz * NC + k], z_recv.at[z * NC + k], (g, zz * 2 + y, c))
+
+    def z_arrived(zz, k):
+        piece = z_in.at[zz, rows_of(k)]
+        remote(piece, piece, z_send.at[0], z_recv.at[zz * NC + k], (g, zz * 2 + y, c)).wait_recv()
 
     back = move_matrix(True)
     for zz in order:
@@ -238,57 +227,36 @@
         at = rows_of(k)
         return part[slot(zz, y, c), at].astype(F32) + sib_in[zz * 2 + y, at].astype(F32) + y_in[zz, at].astype(F32)
 
-    def send_line(copy, out, inn, inner, zz, k):
-        at = rows_of(k)
-        out[zz, at] = mine(zz, k).astype(BF16)
-
-        @pl.when(inner)
-        def _():
-            copy(zz, k).wait_recv()
-            out[zz, at] = (mine_again(zz, k) + inn[zz, at].astype(F32)).astype(BF16)
-
-        copy(zz, k).start()
-
-    def mine_again(zz, k):
-        at = rows_of(k)
-        return part[slot(zz, y, c), at].astype(F32) + sib_in[zz * 2 + y, at].astype(F32) + y_in[zz, at].astype(F32)
-
-    for d in range(NZ - 1, 0, -1):
+    for zz in order[:3]:
         for k in range(NC):
-            pl.when(z + d < NZ)(functools.partial(send_line, zu_copy, zu_out, zu_in, z > 0, z + d, k))
-            pl.when(z - d >= 0)(functools.partial(send_line, zd_copy, zd_out, zd_in, z < NZ - 1, z - d, k))
-    for k in range(NC):
-        out_ref[rows_of(k)] = mine(z, k)
-
-    @pl.when(z > 0)
-    def _():
-        for k in range(NC):
-            zu_copy(z, k).wait_recv()
-            out_ref[rows_of(k)] += zu_in[z, rows_of(k)].astype(F32)
-
-    @pl.when(z < NZ - 1)
-    def _():
-        for k in range(NC):
-            zd_copy(z, k).wait_recv()
-            out_ref[rows_of(k)] += zd_in[z, rows_of(k)].astype(F32)
-
-    def left(copy, zz, k):
-        copy(zz, k).wait_send()
-
-    for zz in range(NZ):
-        for k in range(NC):
-            pl.when((z < NZ - 1) & (zz <= z))(functools.partial(left, to_up, zz, k))
-            pl.when((z > 0) & (zz >= z))(functools.partial(left, to_down, zz, k))
+            z_out[zz, rows_of(k)] = mine(zz, k).astype(BF16)
+            z_copy(zz, k).start()
+    for k in range(NC):
+        total = mine(z, k)
+        for zz in others:
+            z_arrived(zz, k)
+            total += z_in[zz, rows_of(k)].astype(F32)
+        out_ref[rows_of(k)] = total
+
+    for k in range(NC):
+        for zz in others:
+            to_z(zz, k).wait_send()
+            z_copy(zz, k).wait_send()
+        for zz in range(NZ):
             to_y(zz, k).wait_send()
             y_copy(zz, k).wait_send()
             for yy in range(2):
                 to_sib(zz, yy, k).wait_send()
                 s_copy(zz, yy, k).wait_send()
-            pl.when(zz > z)(functools.partial(left, zu_copy, zz, k))
-            pl.when(zz < z)(functools.partial(left, zd_copy, zz, k))
-
-
-def spread_kernel(place_ref, weight_ref, merged_ref, out_hbm, stage, sems):
+
+
+def spread_kernel(place_hbm, weight_hbm, merged_hbm, out_hbm, place_ref, weight_ref, merged_ref, stage, sems):
+    loads = [pltpu.make_async_copy(src, dst, sems.at[PARTS + i]) for i, (src, dst) in enumerate(
+        ((place_hbm, place_ref), (weight_hbm, weight_ref), (merged_hbm, merged_ref)))]
+    for load in loads:
+        load.start()
+    for load in loads:
+        load.wait()
     tok, width = place_ref.shape[0], merged_ref.shape[1]
     place, weight = place_ref[:, :ROWS], weight_ref[:, :1]
     merged = merged_ref[...]
@@ -336,10 +304,9 @@
             blocks(SH),
             pltpu.VMEM((NZ * 32, model), BF16),
             pltpu.VMEM((NZ, PARTS * 32, width), BF16),
-            blocks(SH), blocks(8), blocks(NZ), blocks(NZ), blocks(NZ), blocks(NZ), blocks(NZ), blocks(NZ),
-            dma((6,)), dma((SH * NC,)), dma((NZ * NC,)), dma((NZ * NC,)), dma((NZ * NC,)), dma((8 * NC,)),
-            dma((8 * NC,)), dma((8 * NC,)), dma((NZ * NC,)), dma((NZ * NC,)),
-            dma((NZ * NC,)), dma((NZ * NC,)), dma((NZ * NC,)), dma((NZ * NC,)),
+            blocks(SH), blocks(8), blocks(NZ), blocks(NZ), blocks(NZ), blocks(NZ),
+            dma((6,)), dma((SH * NC,)), dma((NZ * NC,)), dma((NZ * NC,)), dma((8 * NC,)),
+            dma((8 * NC,)), dma((8 * NC,)), dma((NZ * NC,)), dma((NZ * NC,)), dma((NZ * NC,)), dma((NZ * NC,)),
         ],
         compiler_params=pltpu.CompilerParams(
             collective_id=0, has_side_effects=True, vmem_limit_bytes=60 * 1024 * 1024),
@@ -348,10 +315,11 @@
     return pl.pallas_call(
         spread_kernel,
         out_shape=jax.ShapeDtypeStruct((tok, model), BF16),
-        in_specs=[vmem, vmem, vmem],
+        in_specs=[hbm, hbm, hbm],
         out_specs=hbm,
-        scratch_shapes=[pltpu.VMEM((tok, model), BF16), dma((PARTS,))],
-        compiler_params=pltpu.CompilerParams(vmem_limit_bytes=32 * 1024 * 1024),
+        scratch_shapes=[pltpu.VMEM(place.shape, jnp.int32), pltpu.VMEM(weight.shape, F32), pltpu.VMEM(merged.shape, F32),
+                        pltpu.VMEM((tok, model), BF16), dma((PARTS + 3,))],
+        compiler_params=pltpu.CompilerParams(vmem_limit_bytes=60 * 1024 * 1024),
         name="spread",
     )(place, weight, merged)
 

time: 45.3 us -> 39.4 us (0.87)
  Pallas kernels: 42.5 us -> 39.2 us
  local copies, waits for them, and re-layouts: 2.59 us -> 0 us
    pallas_call x1, Pallas kernels: 40 us -> 35.7 us  [fast(): pl.pallas_call(moe_kernel, out_shape=(jax.ShapeDtypeStruct((ROWS, width),...]
    unnamed x6 -> x0, local copies, waits for them, and re-layouts: 2.59 us -> none
    pallas_call x1, Pallas kernels: 2.47 us -> 3.48 us  [fast(): pl.pallas_call(spread_kernel, out_shape=jax.ShapeDtypeStruct((tok, model)...]
where the time goes in v3:
time: 39.4 us; the launch traced here: 39.2 us
  Pallas kernels  39.2 us (99%)
    pallas_call x1, Pallas kernels, fast(): pl.pallas_call(moe_kernel, out_shape=(jax.ShapeDtypeStruct((ROWS, width),...  35.7 us
    pallas_call x1, Pallas kernels, fast(): pl.pallas_call(spread_kernel, out_shape=jax.ShapeDtypeStruct((tok, model)...  3.48 us

profile of v3, /device:TPU:0, one launch (start us, length us, event | category | flops | bytes accessed | tf_op | source)
XLA Modules:
  0.0 39.2 jit_solution(4976377907569967134)
XLA Ops:
  0.0 35.7 %expert.1 = (f32[48,896]{1,0:T(8,128)}, s32[128,128]{1,0:T(8,128)}, f32[128,128]{1,0:T(8,128)}) custom-call(s32[8,128]{1,0:T(8,128)} %bitcast.2, f32[8,128]{1,0:T(8,128)} %bitcast.3, bf16[128,7168]{1,0:T(8,128)(2,1)} %tok_hbm.1, bf16[1,7168,128]{2,1,0:T(8,128)(2,1)} %gate_hbm.1, bf16[1,7168,128]{2,1,0:T(8,128)(2,1)} %up_hbm.1, bf16[1,128,7168]{2,1,0:T(8,128)(2,1)} %down_hbm.1), custom_call_target="tpu_custom_call" | custom-call | tf_op jit(solution)/shard_map/expert/pallas_call | solution.py:292
  35.7 3.5 %spread.1 = bf16[128,7168]{1,0:T(8,128)(2,1)} custom-call(s32[128,128]{1,0:T(8,128)} %get-tuple-element.8.place_hbm, f32[128,128]{1,0:T(8,128)} %get-tuple-element.9.weight_hbm, f32[48,896]{1,0:T(8,128)} %get-tuple-element.10.merged_hbm), custom_call_target="tpu_custom_call" | custom-call | tf_op jit(solution)/shard_map/spread/pallas_call | solution.py:315
